TPU v7x, 32 devices: a whole 2x2x4 slice. The times are simulated.
32 devices in a mesh: query: 2 (over x), corpus: 16 (over z, y, core).
Axes of the slice: x: 2, y: 2, z: 4, core: 2. Of those that a mesh axis runs over, the one named last changes fastest.
Arguments:
- clean_feats: bfloat16 [2, 2, 512, 320], P('query', None, 'corpus'), may hold values from -6 to 6
- noise_draw: bfloat16 [2, 2, 512, 320], P('query', None, 'corpus'), may hold values from -6 to 6
- timesteps: int32 [2, 2], P('query'), may hold values from 0 to 999
- weight_in: bfloat16 [2, 320, 320], P(None, None, 'corpus'), may hold values from -0.3125 to 0.3125
- weight_ffin: bfloat16 [2, 320, 2560], P(None, None, 'corpus'), may hold values from -0.3125 to 0.3125
- weight_ffout: bfloat16 [2, 1280, 320], P(None, None, 'corpus'), may hold values from -0.15625 to 0.15625
- weight_out: bfloat16 [2, 320, 320], P(None, None, 'corpus'), may hold values from -0.3125 to 0.3125
- norm_gain: float32 [2, 320], replicated, may hold values from 0.5 to 1.5
- norm_bias: float32 [2, 320], replicated, may hold values from -3 to 3
- sketch_cin: bfloat16 [2, 3, 320, 16], replicated, may hold values from -0.3125 to 0.3125
- sketch_fin: bfloat16 [2, 1280, 16], replicated, may hold values from -0.15625 to 0.15625
- sketch_cout: bfloat16 [2, 3, 320, 16], replicated, may hold values from -0.3125 to 0.3125
- sketch_fout: bfloat16 [2, 2560, 16], replicated, may hold values from -0.125 to 0.125
- precond: float32 [8, 256, 256], P('query'), as said below
- store_grads: bfloat16 [8192, 2048], P(('query', 'corpus')), may hold values from -6 to 6
- store_scale: float32 [8192], P(('query', 'corpus')), may hold values from 0.002 to 0.03
Outputs:
- scores: float32 [2, 8192], P(None, ('query', 'corpus'))
Inputs may be any that keep to these rules, and one draw needn't show every extreme that they name: `precond`: each layer's matrix is symmetric with a diagonal between 1 and 2.
All inputs are finite; a program needn't handle non-finite values.
Results may differ from a plain program's by a relative error of at most 0.0085.
Values may be sent and summed in bfloat16 or wider, within the bound.
A program may use at most 64 MiB of HBM per device.

v0:
```python
import math
import jax
import jax.numpy as jnp
from jax import lax
from jax.sharding import PartitionSpec as P

plan_len = 1000


def noise_levels(timesteps):
    steps = jnp.arange(plan_len, dtype=jnp.float32)
    rooted = math.sqrt(0.00085) + (math.sqrt(0.012) - math.sqrt(0.00085)) * steps / (plan_len - 1)
    terms = jnp.log1p(-rooted * rooted)
    reached = jnp.arange(plan_len, dtype=jnp.int32) <= timesteps[..., None]
    picked = jnp.exp(jnp.sum(jnp.where(reached, terms, jnp.zeros_like(terms)), axis=-1))
    return (jnp.sqrt(picked), jnp.sqrt(1.0 - picked))


def gelu_parts(gate):
    cumul = 0.5 * (1.0 + jax.scipy.special.erf(gate / math.sqrt(2.0)))
    density = jnp.exp(-0.5 * gate * gate) / math.sqrt(2.0 * math.pi)
    return (gate * cumul, cumul + gate * density)


def contract_back(delta, weight):
    return lax.dot_general(
        delta, weight, (((1,), (1,)), ((), ())), preferred_element_type=jnp.float32
    )


def block_forward(residual_stream, weights, scale_gain, shift_bias):
    weight_in, weight_ffin, weight_ffout, weight_out = weights
    hidden = weight_ffout.shape[0]
    residual_reduced = residual_stream.astype(jnp.bfloat16)
    inner = jnp.dot(residual_reduced, weight_in, preferred_element_type=jnp.float32)
    centred_input = inner - jnp.mean(inner, axis=-1, keepdims=True)
    inverse_deviation = lax.rsqrt(
        jnp.mean(centred_input * centred_input, axis=-1, keepdims=True) + 1e-05
    )
    standardized_input = centred_input * inverse_deviation
    normalized_input = (standardized_input * scale_gain + shift_bias).astype(jnp.bfloat16)
    projected = jnp.dot(normalized_input, weight_ffin, preferred_element_type=jnp.float32)
    value_output = projected[:, :hidden]
    gate = projected[:, hidden:]
    gelu_result, gelu_derivative = gelu_parts(gate)
    mixed_hidden = (value_output * gelu_result).astype(jnp.bfloat16)
    inner_two = inner + jnp.dot(mixed_hidden, weight_ffout, preferred_element_type=jnp.float32)
    inner_reduced = inner_two.astype(jnp.bfloat16)
    residual_stream = residual_stream + jnp.dot(
        inner_reduced, weight_out, preferred_element_type=jnp.float32
    )
    return (
        residual_stream,
        (
            residual_reduced,
            standardized_input,
            inverse_deviation,
            normalized_input,
            value_output,
            gelu_result,
            gelu_derivative,
            mixed_hidden,
            inner_reduced,
        ),
    )


def block_backward(dstream, saved_activations, weights, scale_gain):
    weight_in, weight_ffin, weight_ffout, weight_out = weights
    (
        residual_reduced,
        standardized_input,
        inverse_deviation,
        normalized_input,
        value_output,
        gelu_result,
        gelu_derivative,
        mixed_hidden,
        inner_reduced,
    ) = saved_activations
    dout_low = dstream.astype(jnp.bfloat16)
    second_inner_gradient = contract_back(dout_low, weight_out)
    dtwo_low = second_inner_gradient.astype(jnp.bfloat16)
    dmixed = contract_back(dtwo_low, weight_ffout)
    dproj_low = jnp.concatenate(
        [dmixed * gelu_result, dmixed * value_output * gelu_derivative], axis=-1
    ).astype(jnp.bfloat16)
    dnormed = contract_back(dproj_low, weight_ffin)
    scaled_hidden = dnormed * scale_gain
    inner_gradient = second_inner_gradient + inverse_deviation * (
        scaled_hidden
        - jnp.mean(scaled_hidden, axis=-1, keepdims=True)
        - standardized_input * jnp.mean(scaled_hidden * standardized_input, axis=-1, keepdims=True)
    )
    dinner_low = inner_gradient.astype(jnp.bfloat16)
    dstream = dstream + contract_back(dinner_low, weight_in)
    records = [
        (residual_reduced, dinner_low),
        (normalized_input, dproj_low),
        (mixed_hidden, dtwo_low),
        (inner_reduced, dout_low),
    ]
    return (dstream, records)


def project_layer(inputs, deltas, sketch_in, sketch_out, samples):
    left = jnp.dot(inputs, sketch_in, preferred_element_type=jnp.float32)
    right = jnp.dot(deltas, sketch_out, preferred_element_type=jnp.float32)
    left = left.reshape(samples, -1, left.shape[-1])
    right = right.reshape(samples, -1, right.shape[-1])
    outer = jnp.einsum("srk,srj->skj", left, right, precision=lax.Precision.HIGHEST)
    return outer.reshape(samples, -1)


def sketches_of(block, sketch_cin, sketch_fin, sketch_cout, sketch_fout):
    return [
        (sketch_cin[block, 0], sketch_cout[block, 0]),
        (sketch_cin[block, 1], sketch_fout[block]),
        (sketch_fin[block], sketch_cout[block, 1]),
        (sketch_cin[block, 2], sketch_cout[block, 2]),
    ]


def on_device(
    clean_feats,
    noise_draw,
    timesteps,
    weight_in,
    weight_ffin,
    weight_ffout,
    weight_out,
    norm_gain,
    norm_bias,
    sketch_cin,
    sketch_fin,
    sketch_cout,
    sketch_fout,
    precond,
    store_grads,
    store_scale,
):
    samples = clean_feats.shape[0]
    positions = clean_feats.shape[2] * lax.axis_size("corpus")
    loss_scale = 1.0 / math.sqrt(clean_feats.shape[1] * positions)
    blocks = weight_in.shape[0]
    signal, spread = noise_levels(timesteps)
    noise_rows = noise_draw.astype(jnp.float32)
    residual_stream = (
        signal[:, :, None, None] * clean_feats.astype(jnp.float32)
        + spread[:, :, None, None] * noise_rows
    )
    residual_stream = residual_stream.reshape(-1, residual_stream.shape[-1])
    noise_rows = noise_rows.reshape(-1, noise_rows.shape[-1])
    gathered = (
        lax.all_gather(weight_in, "corpus", axis=2, tiled=True),
        lax.all_gather(weight_ffin, "corpus", axis=2, tiled=True),
        lax.all_gather(weight_ffout, "corpus", axis=2, tiled=True),
        lax.all_gather(weight_out, "corpus", axis=2, tiled=True),
    )

    def fetch_forward(block):
        return tuple((member[block] for member in gathered))

    def fetch_backward(block):
        return tuple((member[block] for member in gathered))

    saved_all = []
    for block in range(blocks):
        residual_stream, saved_activations = block_forward(
            residual_stream, fetch_forward(block), norm_gain[block], norm_bias[block]
        )
        saved_all.append(saved_activations)
    dstream = (residual_stream - noise_rows) * loss_scale
    layers = [None] * (4 * blocks)
    for block in reversed(range(blocks)):
        dstream, records = block_backward(
            dstream, saved_all[block], fetch_backward(block), norm_gain[block]
        )
        pairs = sketches_of(block, sketch_cin, sketch_fin, sketch_cout, sketch_fout)
        for index in range(4):
            layers[4 * block + index] = project_layer(
                records[index][0], records[index][1], pairs[index][0], pairs[index][1], samples
            )
    partial_grads = jnp.stack(layers, axis=1)
    totals = lax.psum(partial_grads, "corpus")
    routed = lax.all_to_all(totals, "query", split_axis=1, concat_axis=0, tiled=True)
    owned = jnp.einsum("qlk,lkj->qlj", routed, precond, precision=lax.Precision.HIGHEST).astype(
        jnp.bfloat16
    )
    preconditioned = lax.all_gather(owned, "query", axis=1, tiled=True)
    flat = preconditioned.reshape(preconditioned.shape[0], -1)
    raw = lax.dot_general(
        flat, store_grads, (((1,), (1,)), ((), ())), preferred_element_type=jnp.float32
    )
    return raw * store_scale[None, :]


def solution(mesh):
    placed = (
        P("query", None, "corpus", None),
        P("query", None, "corpus", None),
        P("query", None),
        P(None, None, "corpus"),
        P(None, None, "corpus"),
        P(None, None, "corpus"),
        P(None, None, "corpus"),
        P(),
        P(),
        P(),
        P(),
        P(),
        P(),
        P("query", None, None),
        P(("query", "corpus"), None),
        P(("query", "corpus")),
    )
    return jax.shard_map(
        on_device,
        mesh=mesh,
        in_specs=placed,
        out_specs=P(None, ("query", "corpus")),
        check_vma=False,
    )
```

profile of v0, /device:TPU:0, one launch (start us, length us, event | category | flops | bytes accessed | tf_op | source)
XLA Modules:
  0.0 167.8 jit_solution(465755251760985908)
XLA Ops:
  6.5 0.7 all-gather.5.cloned.1.call-update
  7.3 0.7 all-gather.3.cloned.1.call-update
  8.0 25.0 %all_gather.15 = bf16[2,320,320]{1,0,2:T(2,128)(2,1)S(1)} all-gather(bf16[2,320,20]{1,0,2:T(2,128)(2,1)} %param.19), channel_id=1, replica_groups=mesh['query'=2,'corpus'=16] {'corpus'}, dimensions={2}, use_global_device_ids=true | all-gather | bytes 435200 | tf_op jit(solution)/shard_map/all_gather | solution.py:155
  33.0 0.7 fusion.105
  33.7 0.9 copy.52
  34.6 19.7 %all_gather.18 = bf16[2,320,320]{1,0,2:T(2,128)(2,1)S(1)} all-gather(bf16[2,320,20]{1,0,2:T(2,128)(2,1)S(1)} %copy-done.12), channel_id=1, replica_groups=mesh['query'=2,'corpus'=16] {'corpus'}, dimensions={2}, use_global_device_ids=true | all-gather | bytes 435200 | tf_op jit(solution)/shard_map/all_gather | solution.py:158
  54.3 0.7 fusion.104
  55.0 0.9 copy.54
  55.9 0.9 copy.55
  56.8 0.9 copy.57
  57.7 0.6 slice_reduce_fusion
  58.6 0.7 fusion.102
  59.3 0.3 fusion.106
  59.8 0.8 fusion.79
  60.7 0.6 copy-done.4
  61.3 0.8 fusion.76
  62.2 5.7 %fusion.103 = (bf16[1,1280,320]{1,0,2:T(2,128)(2,1)}, bf16[1,1280,320]{1,0,2:T(2,128)(2,1)S(1)}) fusion(bf16[2,1280,320]{1,0,2:T(2,128)(2,1)} %all-gather.5.cloned.1.call-done), kind=kLoop, calls=%fused_computation.161 | loop fusion | bytes 3276800 | tf_op jit(solution)/shard_map/slice | solution.py:162
  67.9 36.5 %all-gather.3.cloned.1.call-done = bf16[2,320,2560]{1,2,0:T(8,128)(2,1)} async-done(((bf16[2,320,160]{1,2,0:T(8,128)(2,1)}), bf16[2,320,2560]{1,2,0:T(8,128)(2,1)}) %all-gather.3.cloned.1.call-update) | async-done | bytes 3276816 | tf_op jit(solution)/shard_map/all_gather | solution.py:156
  104.3 2.5 %fusion.1 = f32[64,2560]{1,0:T(8,128)S(1)} fusion(bf16[64,320]{1,0:T(8,128)(2,1)} %copy-done.4, bf16[2,320,2560]{1,2,0:T(8,128)(2,1)} %all-gather.3.cloned.1.call-done), kind=kOutput, calls=%fused_computation.3 | convolution fusion | flops 104857600 | bytes 2670592 | tf_op jit(solution)/shard_map/dot_general | solution.py:42
  106.9 0.4 fusion.8
  108.2 0.7 fusion.3
  109.0 0.3 copy-done.2
  109.3 0.4 fusion.9
  110.1 0.3 multiply_convert_fusion.1
  110.4 0.5 fusion.101
  111.5 0.3 multiply_convert_fusion
  113.7 0.5 fusion.100
  116.3 32.2 %psum.7 = f32[1,8,256]{2,0,1:T(1,128)S(1)} all-reduce(f32[1,8,256]{2,0,1:T(1,128)S(1)} %constant_dynamic-update-slice_fusion), channel_id=1, replica_groups=mesh['query'=2,'corpus'=16] {'corpus'}, use_global_device_ids=true, to_apply=%region_9.10 | all-reduce | flops 2048 | bytes 16384 | tf_op jit(solution)/shard_map/psum | solution.py:185
  148.6 6.3 %all_to_all.12 = f32[1,8,256]{2,0,1:T(1,128)S(1)} all-to-all(f32[1,8,256]{2,0,1:T(1,128)S(1)} %psum.7), channel_id=1, replica_groups=mesh['query'=2,'corpus'=16] {'query'}, dimensions={1} | all-to-all | bytes 16384 | tf_op jit(solution)/shard_map/all_to_all | solution.py:186
  155.0 0.6 fusion.11
  155.6 4.3 %all_gather.19 = bf16[2,8,256]{2,0,1:T(2,128)(2,1)S(1)} all-gather(bf16[2,4,256]{2,0,1:T(2,128)(2,1)S(1)} %fusion.11), channel_id=1, replica_groups=mesh['query'=2,'corpus'=16] {'query'}, dimensions={1}, use_global_device_ids=true | all-gather | bytes 12288 | tf_op jit(solution)/shard_map/all_gather | solution.py:190
  160.0 1.0 convolution_multiply_fusion
  (111 shorter events, 6.5 us)
Async XLA Ops:
  6.5 148.5 %copy-start = (f32[4,256,256]{2,1,0:T(8,128)S(1)}, f32[4,256,256]{2,1,0:T(8,128)}, u32[]{:S(2)}) copy-start(f32[4,256,256]{2,1,0:T(8,128)} %param.29) | copy-start | bytes 3145732
  6.5 28.1 %copy-start.12 = (bf16[2,320,20]{1,0,2:T(2,128)(2,1)S(1)}, bf16[2,320,20]{1,0,2:T(2,128)(2,1)}, u32[]{:S(2)}) copy-start(bf16[2,320,20]{1,0,2:T(2,128)(2,1)} %param.22) | copy-start | bytes 76804
  6.5 55.6 %all-gather.5.cloned.1.call-start = ((), (), s32[]{:S(2)}) async-start(), calls=%async_computation.2 | async-start | bytes 1740800 | tf_op jit(solution)/shard_map/all_gather | solution.py:157
  7.3 97.1 %all-gather.3.cloned.1.call-start = ((), (), s32[]{:S(2)}) async-start(), calls=%async_computation.1 | async-start | bytes 4177920 | tf_op jit(solution)/shard_map/all_gather | solution.py:156
  54.3 3.4 %copy-start.16 = (f32[2,320]{1,0:T(2,128)S(1)}, f32[2,320]{1,0:T(2,128)}, u32[]{:S(2)}) copy-start(f32[2,320]{1,0:T(2,128)} %param.24) | copy-start | bytes 7684
  54.3 4.0 %copy-start.17 = (f32[2,320]{1,0:T(2,128)S(1)}, f32[2,320]{1,0:T(2,128)}, u32[]{:S(2)}) copy-start(f32[2,320]{1,0:T(2,128)} %param.23) | copy-start | bytes 7684
  54.3 4.0 %copy-start.21 = (s32[1,2]{1,0:T(1,128)S(1)}, s32[1,2]{1,0:T(1,128)}, u32[]{:S(2)}) copy-start(s32[1,2]{1,0:T(1,128)} %param.18) | copy-start | bytes 28
  54.3 4.3 %copy-start.6 = (bf16[1,2,32,320]{3,2,1,0:T(8,128)(2,1)S(1)}, bf16[1,2,32,320]{3,2,1,0:T(8,128)(2,1)}, u32[]{:S(2)}) copy-start(bf16[1,2,32,320]{3,2,1,0:T(8,128)(2,1)} %param.17) | copy-start | bytes 122884
  54.3 4.3 %copy-start.11 = (bf16[1,2,32,320]{3,2,1,0:T(8,128)(2,1)S(1)}, bf16[1,2,32,320]{3,2,1,0:T(8,128)(2,1)}, u32[]{:S(2)}) copy-start(bf16[1,2,32,320]{3,2,1,0:T(8,128)(2,1)} %param.16) | copy-start | bytes 122884
  59.6 8.3 %copy-start.14 = (f32[64]{0:T(128)}, f32[64]{0:T(128)S(1)}, u32[]{:S(2)}) copy-start(f32[64]{0:T(128)S(1)} %broadcast_multiply_fusion.5) | copy-start | bytes 772
  59.8 2.4 %copy-start.18 = (f32[64]{0:T(128)}, f32[64]{0:T(128)S(1)}, u32[]{:S(2)}) copy-start(f32[64]{0:T(128)S(1)} %add_rsqrt_fusion.1) | copy-start | bytes 772
  60.7 0.6 copy-start.4
  104.3 2.9 %copy-start.10 = (bf16[2,3,320,16]{2,3,1,0:T(8,128)(2,1)S(1)}, bf16[2,3,320,16]{2,3,1,0:T(8,128)(2,1)}, u32[]{:S(2)}) copy-start(bf16[2,3,320,16]{2,3,1,0:T(8,128)(2,1)} %param.25) | copy-start | bytes 184324
  104.3 3.1 %copy-start.5 = (f32[1,2,32,320]{3,2,1,0:T(8,128)S(1)}, f32[1,2,32,320]{3,2,1,0:T(8,128)}, u32[]{:S(2)}) copy-start(f32[1,2,32,320]{3,2,1,0:T(8,128)} %get-tuple-element.14) | copy-start | bytes 245764
  104.3 3.9 %copy-start.1 = (bf16[2,320,2560]{1,2,0:T(8,128)(2,1)S(1)}, bf16[2,320,2560]{1,2,0:T(8,128)(2,1)}, u32[]{:S(2)}) copy-start(bf16[2,320,2560]{1,2,0:T(8,128)(2,1)} %all-gather.3.cloned.1.call-done) | copy-start | bytes 9830404
  106.8 1.3 copy-start.13
  107.9 1.4 copy-start.2
  108.2 1.5 copy-start.7
  110.9 0.9 copy-start.9
  110.9 1.6 copy-start.8
  111.3 2.0 %copy-start.22 = (bf16[2,2560,16]{1,2,0:T(8,128)(2,1)S(1)}, bf16[2,2560,16]{1,2,0:T(8,128)(2,1)}, u32[]{:S(2)}) copy-start(bf16[2,2560,16]{1,2,0:T(8,128)(2,1)} %param.28) | copy-start | bytes 491524
  111.5 2.2 %copy-start.15 = (f32[64]{0:T(128)S(1)}, f32[64]{0:T(128)}, u32[]{:S(2)}) copy-start(f32[64]{0:T(128)} %copy-done.14) | copy-start | bytes 772
  111.5 2.2 %copy-start.19 = (f32[64]{0:T(128)S(1)}, f32[64]{0:T(128)}, u32[]{:S(2)}) copy-start(f32[64]{0:T(128)} %copy-done.18) | copy-start | bytes 772
  113.7 46.3 %copy-start.3 = (bf16[256,2048]{1,0:T(8,128)(2,1)S(1)}, bf16[256,2048]{1,0:T(8,128)(2,1)}, u32[]{:S(2)}) copy-start(bf16[256,2048]{1,0:T(8,128)(2,1)} %param.30) | copy-start | bytes 3145732
  113.7 46.3 %copy-start.20 = (f32[256]{0:T(256)S(1)}, f32[256]{0:T(256)}, u32[]{:S(2)}) copy-start(f32[256]{0:T(256)} %param.31) | copy-start | bytes 3076
Sparse Core Ops, SparseCore 0:
  9.5 43.8 all-gather.4
  55.7 48.5 all-gather.2
where the time goes:
time: 168 us
  blocking collectives  87.6 us (52%)
  waiting for transfers between devices  37.9 us (23%)
  between operations  13.9 us (8%)
  matrix products  13.5 us (8%)
  local copies, waits for them, and re-layouts  13 us (8%)
  other arithmetic  1.84 us (1%)
    all_gather x1, waiting for transfers between devices, on_device(): lax.all_gather(weight_ffin, 'corpus', axis=2, tiled=True)  36.5 us
    psum x1, blocking collectives, on_device(): totals = lax.psum(partial_grads, 'corpus')  32.2 us
    all_gather x1, blocking collectives, on_device(): lax.all_gather(weight_in, 'corpus', axis=2, tiled=True)  25 us
    all_gather x1, blocking collectives, on_device(): lax.all_gather(weight_out, 'corpus', axis=2, tiled=True)  19.7 us
    slice x3, local copies, waits for them, and re-layouts, fetch_forward(): return tuple((member[block] for member in gathered))  7.04 us
    all_to_all x1, blocking collectives, on_device(): lax.all_to_all(totals, 'query', split_axis=1, concat_axis=0, tiled=True)  6.35 us
    unnamed x57, local copies, waits for them, and re-layouts  4.61 us
    all_gather x1, blocking collectives, on_device(): preconditioned = lax.all_gather(owned, 'query', axis=1, tiled=True)  4.33 us
  transfers between devices with their start and end apart: 2, of which 1 were waited for; matrix products, arithmetic and copies ran while one was open for 9% of the time, Pallas kernels for 0%

commit v1 on v0

--- a/solution.py
+++ b/solution.py
@@ -5,6 +5,18 @@
 from jax.sharding import PartitionSpec as P
 
 plan_len = 1000
+
+
+def collect(x, axis, dim):
+    ways, here = (lax.axis_size(axis), lax.axis_index(axis))
+    grown, reach = (x, 1)
+    while reach < ways:
+        theirs = lax.ppermute(grown, axis, [(d, d ^ reach) for d in range(ways)])
+        mine_first = jnp.concatenate([grown, theirs], axis=dim)
+        theirs_first = jnp.concatenate([theirs, grown], axis=dim)
+        grown = jnp.where(here & reach == 0, mine_first, theirs_first)
+        reach = 2 * reach
+    return grown
 
 
 def noise_levels(timesteps):
@@ -153,7 +165,7 @@
     noise_rows = noise_rows.reshape(-1, noise_rows.shape[-1])
     gathered = (
         lax.all_gather(weight_in, "corpus", axis=2, tiled=True),
-        lax.all_gather(weight_ffin, "corpus", axis=2, tiled=True),
+        collect(weight_ffin, "corpus", 2),
         lax.all_gather(weight_ffout, "corpus", axis=2, tiled=True),
         lax.all_gather(weight_out, "corpus", axis=2, tiled=True),
     )

time: 168 us -> 229 us (1.36)
  waiting for transfers between devices: 37.9 us -> 62.3 us
  blocking collectives: 87.6 us -> 109 us
  other arithmetic: 1.84 us -> 7.9 us
  local copies, waits for them, and re-layouts: 13 us -> 18.7 us
  starting transfers between devices: 0.04 us -> 3.62 us
    ppermute x0 -> x4, waiting for transfers between devices: none -> 62.3 us  [collect(): theirs = lax.ppermute(grown, axis, [(d, d ^ reach) for d in range(ways)])]
    all_gather x1 -> x0, waiting for transfers between devices: 36.5 us -> none  [on_device(): lax.all_gather(weight_ffin, 'corpus', axis=2, tiled=True)]
    all_gather x1, blocking collectives: 19.7 us -> 37.9 us  [on_device(): lax.all_gather(weight_out, 'corpus', axis=2, tiled=True)]
    select_n x0 -> x4, other arithmetic: none -> 5.39 us  [collect(): grown = jnp.where(here & reach == 0, mine_first, theirs_first)]
    all_gather x1, blocking collectives: 25 us -> 30.4 us  [on_device(): lax.all_gather(weight_in, 'corpus', axis=2, tiled=True)]
    unnamed x57 -> x60, local copies, waits for them, and re-layouts: 4.61 us -> 9.49 us
    ppermute x0 -> x4, starting transfers between devices: none -> 3.62 us  [collect(): theirs = lax.ppermute(grown, axis, [(d, d ^ reach) for d in range(ways)])]
    dot_general x2, matrix products: 3.18 us -> 0.87 us  [block_forward(): jnp.dot(normalized_input, weight_ffin, preferred_element_type=jnp.float32)]
  transfers between devices with their start and end apart: 2 -> 5, of which waited for: 1 -> 2; matrix products, arithmetic and copies ran while one was open for 9% -> 9% of each run, Pallas kernels for 0% -> 0%
where the time goes in v1:
time: 229 us
  blocking collectives  109 us (48%)
  waiting for transfers between devices  62.3 us (27%)
  local copies, waits for them, and re-layouts  18.7 us (8%)
  between operations  13.9 us (6%)
  matrix products  13.3 us (6%)
  other arithmetic  7.9 us (3%)
  starting transfers between devices  3.62 us (2%)
    ppermute x4, waiting for transfers between devices, collect(): theirs = lax.ppermute(grown, axis, [(d, d ^ reach) for d in range(ways)])  62.3 us
    all_gather x1, blocking collectives, on_device(): lax.all_gather(weight_out, 'corpus', axis=2, tiled=True)  37.9 us
    all_gather x1, blocking collectives, on_device(): lax.all_gather(weight_in, 'corpus', axis=2, tiled=True)  30.4 us
    psum x1, blocking collectives, on_device(): totals = lax.psum(partial_grads, 'corpus')  30.2 us
    unnamed x60, local copies, waits for them, and re-layouts  9.49 us
    slice x3, local copies, waits for them, and re-layouts, fetch_forward(): return tuple((member[block] for member in gathered))  7.84 us
    all_to_all x1, blocking collectives, on_device(): lax.all_to_all(totals, 'query', split_axis=1, concat_axis=0, tiled=True)  6.35 us
    select_n x4, other arithmetic, collect(): grown = jnp.where(here & reach == 0, mine_first, theirs_first)  5.39 us
  transfers between devices with their start and end apart: 5, of which 2 were waited for; matrix products, arithmetic and copies ran while one was open for 9% of the time, Pallas kernels for 0%

profile of v1, /device:TPU:0, one launch (start us, length us, event | category | flops | bytes accessed | tf_op | source)
XLA Modules:
  0.0 228.9 jit_solution(3959445959421087402)
XLA Ops:
  6.5 1.2 copy.41
  7.8 0.5 collective-permute-start
  8.3 0.8 fusion.93
  10.0 3.0 %collective-permute-start.1 = (bf16[2,320,320]{2,1,0:T(8,128)(2,1)S(1)}, bf16[2,320,320]{2,1,0:T(8,128)(2,1)S(1)}, u32[]{:S(2)}, u32[]{:S(2)}) collective-permute-start(bf16[2,320,320]{2,1,0:T(8,128)(2,1)S(1)} %maximum_select_fusion.3), channel_id=1, source_target_pairs={{0,2},{1,3},{2,0},{3,1},{4,6},{5,7},{6,4},{7,5},{8,10},{9,11},{10,... | collective-permute-start | bytes 1228808 | tf_op jit(solution)/shard_map/ppermute | solution.py:14
  12.9 30.4 %all_gather.12 = bf16[2,320,320]{1,0,2:T(2,128)(2,1)S(1)} all-gather(bf16[2,320,20]{1,0,2:T(2,128)(2,1)S(1)} %copy-done.13), channel_id=1, replica_groups=mesh['query'=2,'corpus'=16] {'corpus'}, dimensions={2}, use_global_device_ids=true | all-gather | bytes 435200 | tf_op jit(solution)/shard_map/all_gather | solution.py:167
  43.3 0.6 maximum_select_fusion.2
  44.0 37.9 %all_gather.14 = bf16[2,320,320]{1,0,2:T(2,128)(2,1)S(1)} all-gather(bf16[2,320,20]{1,0,2:T(2,128)(2,1)S(1)} %copy-done.14), channel_id=1, replica_groups=mesh['query'=2,'corpus'=16] {'corpus'}, dimensions={2}, use_global_device_ids=true | all-gather | bytes 435200 | tf_op jit(solution)/shard_map/all_gather | solution.py:170
  81.9 0.8 fusion.102
  82.6 1.6 fusion.105
  84.3 1.7 fusion.104
  85.9 1.8 maximum_select_fusion.1
  87.8 2.0 copy.58
  89.8 1.5 copy.60
  91.3 1.5 copy.61
  92.8 1.5 copy.63
  94.3 0.6 slice_reduce_fusion.1
  94.9 1.2 fusion.106
  96.4 0.9 fusion.79
  97.4 0.8 fusion.76
  98.2 61.9 %collective-permute-done.3 = bf16[2,320,1280]{2,1,0:T(8,128)(2,1)} collective-permute-done((bf16[2,320,1280]{2,1,0:T(8,128)(2,1)S(1)}, bf16[2,320,1280]{2,1,0:T(8,128)(2,1)}, u32[]{:S(2)}, u32[]{:S(2)}) %collective-permute-start.3) | collective-permute-done | bytes 1638432 | tf_op jit(solution)/shard_map/ppermute | solution.py:14
  160.2 2.6 %maximum_select_fusion = bf16[2,320,2560]{2,1,0:T(8,128)(2,1)S(1)} fusion(bf16[2,320,1280]{2,1,0:T(8,128)(2,1)} %collective-permute-done.3, bf16[2,320,1280]{2,1,0:T(8,128)(2,1)S(1)} %maximum_select_fusion.1, pred[]{:T(512)S(6)} %eq.12), kind=kLoop, calls=%fused_computation | loop fusion | flops 14745600 | bytes 6553601 | tf_op jit(solution)/shard_map/jit(_where)/select_n | solution.py:17
  162.8 1.7 copy-done.1
  164.5 0.4 fusion.1
  165.1 4.5 %fusion.103 = (bf16[1,1280,320]{1,0,2:T(2,128)(2,1)S(1)}, bf16[1,1280,320]{1,0,2:T(2,128)(2,1)S(1)}) fusion(bf16[2,1280,320]{1,0,2:T(2,128)(2,1)} %all-gather.2.cloned.1.call-done), kind=kLoop, calls=%fused_computation.165 | loop fusion | bytes 3276800 | tf_op jit(solution)/shard_map/slice | solution.py:174
  172.6 0.7 fusion.101
  174.9 0.7 fusion.100
  176.4 0.8 fusion.63
  179.5 30.2 %psum.7 = f32[1,8,256]{2,0,1:T(1,128)S(1)} all-reduce(f32[1,8,256]{2,0,1:T(1,128)S(1)} %constant_dynamic-update-slice_fusion), channel_id=1, replica_groups=mesh['query'=2,'corpus'=16] {'corpus'}, use_global_device_ids=true, to_apply=%region_9.10 | all-reduce | flops 2048 | bytes 16384 | tf_op jit(solution)/shard_map/psum | solution.py:197
  209.8 6.4 %all_to_all.12 = f32[1,8,256]{2,0,1:T(1,128)S(1)} all-to-all(f32[1,8,256]{2,0,1:T(1,128)S(1)} %psum.7), channel_id=1, replica_groups=mesh['query'=2,'corpus'=16] {'query'}, dimensions={1} | all-to-all | bytes 16384 | tf_op jit(solution)/shard_map/all_to_all | solution.py:198
  216.2 0.6 fusion.11
  216.8 4.3 %all_gather.15 = bf16[2,8,256]{2,0,1:T(2,128)(2,1)S(1)} all-gather(bf16[2,4,256]{2,0,1:T(2,128)(2,1)S(1)} %fusion.11), channel_id=1, replica_groups=mesh['query'=2,'corpus'=16] {'query'}, dimensions={1}, use_global_device_ids=true | all-gather | bytes 12288 | tf_op jit(solution)/shard_map/all_gather | solution.py:202
  221.1 1.0 convolution_multiply_fusion
  (123 shorter events, 8.9 us)
Async XLA Ops:
  6.5 209.6 %copy-start = (f32[4,256,256]{2,1,0:T(8,128)S(1)}, f32[4,256,256]{2,1,0:T(8,128)}, u32[]{:S(2)}) copy-start(f32[4,256,256]{2,1,0:T(8,128)} %param.29) | copy-start | bytes 3145732
  6.5 6.4 %copy-start.13 = (bf16[2,320,20]{1,0,2:T(2,128)(2,1)S(1)}, bf16[2,320,20]{1,0,2:T(2,128)(2,1)}, u32[]{:S(2)}) copy-start(bf16[2,320,20]{1,0,2:T(2,128)(2,1)} %param.19) | copy-start | bytes 76804
  6.5 158.5 %all-gather.2.cloned.1.call-start = ((), (), s32[]{:S(2)}) async-start(), calls=%async_computation.1 | async-start | bytes 1740800 | tf_op jit(solution)/shard_map/all_gather | solution.py:169
  7.8 1.8 collective-permute-start
  9.2 34.8 %copy-start.14 = (bf16[2,320,20]{1,0,2:T(2,128)(2,1)S(1)}, bf16[2,320,20]{1,0,2:T(2,128)(2,1)}, u32[]{:S(2)}) copy-start(bf16[2,320,20]{1,0,2:T(2,128)(2,1)} %param.22) | copy-start | bytes 76804
  9.9 71.9 %copy-start.7 = (bf16[1,2,32,320]{3,2,1,0:T(8,128)(2,1)S(1)}, bf16[1,2,32,320]{3,2,1,0:T(8,128)(2,1)}, u32[]{:S(2)}) copy-start(bf16[1,2,32,320]{3,2,1,0:T(8,128)(2,1)} %param.17) | copy-start | bytes 122884
  10.0 71.9 %copy-start.12 = (bf16[1,2,32,320]{3,2,1,0:T(8,128)(2,1)S(1)}, bf16[1,2,32,320]{3,2,1,0:T(8,128)(2,1)}, u32[]{:S(2)}) copy-start(bf16[1,2,32,320]{3,2,1,0:T(8,128)(2,1)} %param.16) | copy-start | bytes 122884
  10.0 33.3 %collective-permute-start.1 = (bf16[2,320,320]{2,1,0:T(8,128)(2,1)S(1)}, bf16[2,320,320]{2,1,0:T(8,128)(2,1)S(1)}, u32[]{:S(2)}, u32[]{:S(2)}) collective-permute-start(bf16[2,320,320]{2,1,0:T(8,128)(2,1)S(1)} %maximum_select_fusion.3), channel_id=1, source_target_pairs={{0,2},{1,3},{2,0},{3,1},{4,6},{5,7},{6,4},{7,5},{8,10},{9,11},{10,... | collective-permute-start | bytes 1228808 | tf_op jit(solution)/shard_map/ppermute | solution.py:14
  43.9 42.0 %collective-permute-start.2 = (bf16[2,320,640]{2,1,0:T(8,128)(2,1)S(1)}, bf16[2,320,640]{2,1,0:T(8,128)(2,1)}, u32[]{:S(2)}, u32[]{:S(2)}) collective-permute-start(bf16[2,320,640]{2,1,0:T(8,128)(2,1)S(1)} %maximum_select_fusion.2), channel_id=1, source_target_pairs={{0,4},{1,5},{2,6},{3,7},{4,0},{5,1},{6,2},{7,3},{8,12},{9,13},{10,... | collective-permute-start | bytes 2457608 | tf_op jit(solution)/shard_map/ppermute | solution.py:14
  85.9 1.9 copy-start.18
  87.7 6.6 %copy-start.19 = (f32[2,320]{1,0:T(2,128)S(1)}, f32[2,320]{1,0:T(2,128)}, u32[]{:S(2)}) copy-start(f32[2,320]{1,0:T(2,128)} %param.23) | copy-start | bytes 7684
  87.7 72.4 %collective-permute-start.3 = (bf16[2,320,1280]{2,1,0:T(8,128)(2,1)S(1)}, bf16[2,320,1280]{2,1,0:T(8,128)(2,1)}, u32[]{:S(2)}, u32[]{:S(2)}) collective-permute-start(bf16[2,320,1280]{2,1,0:T(8,128)(2,1)S(1)} %maximum_select_fusion.1), channel_id=1, source_target_pairs={{0,8},{1,9},{2,10},{3,11},{4,12},{5,13},{6,14},{7,15},{8,0},{9,1},... | collective-permute-start | bytes 4915208 | tf_op jit(solution)/shard_map/ppermute | solution.py:14
  96.1 1.1 copy-start.16
  96.3 66.5 %copy-start.20 = (f32[64]{0:T(128)}, f32[64]{0:T(128)S(1)}, u32[]{:S(2)}) copy-start(f32[64]{0:T(128)S(1)} %add_rsqrt_fusion.1) | copy-start | bytes 772
  162.8 1.7 copy-start.1
  165.0 4.6 %copy-start.4 = (bf16[64,1280]{1,0:T(8,128)(2,1)}, bf16[64,1280]{1,0:T(8,128)(2,1)S(1)}, u32[]{:S(2)}) copy-start(bf16[64,1280]{1,0:T(8,128)(2,1)S(1)} %multiply_convert_fusion.3) | copy-start | bytes 491524
  165.0 5.0 %copy-start.11 = (bf16[2,3,320,16]{2,3,1,0:T(8,128)(2,1)S(1)}, bf16[2,3,320,16]{2,3,1,0:T(8,128)(2,1)}, u32[]{:S(2)}) copy-start(bf16[2,3,320,16]{2,3,1,0:T(8,128)(2,1)} %param.25) | copy-start | bytes 184324
  165.0 5.1 %copy-start.6 = (f32[1,2,32,320]{3,2,1,0:T(8,128)S(1)}, f32[1,2,32,320]{3,2,1,0:T(8,128)}, u32[]{:S(2)}) copy-start(f32[1,2,32,320]{3,2,1,0:T(8,128)} %get-tuple-element.14) | copy-start | bytes 245764
  165.1 5.9 %copy-start.2 = (bf16[2,320,2560]{2,1,0:T(8,128)(2,1)S(1)}, bf16[2,320,2560]{2,1,0:T(8,128)(2,1)}, u32[]{:S(2)}) copy-start(bf16[2,320,2560]{2,1,0:T(8,128)(2,1)} %copy-done.1) | copy-start | bytes 9830404
  169.6 1.2 copy-start.15
  170.9 0.9 copy-start.8
  173.3 0.9 copy-start.10
  173.4 1.4 copy-start.17
  173.4 1.4 copy-start.21
  174.2 1.4 copy-start.23
  174.8 1.1 copy-start.5
  174.8 1.1 copy-start.9
  175.8 45.3 %copy-start.3 = (bf16[256,2048]{1,0:T(8,128)(2,1)S(1)}, bf16[256,2048]{1,0:T(8,128)(2,1)}, u32[]{:S(2)}) copy-start(bf16[256,2048]{1,0:T(8,128)(2,1)} %param.30) | copy-start | bytes 3145732
  175.8 45.3 %copy-start.22 = (f32[256]{0:T(256)S(1)}, f32[256]{0:T(256)}, u32[]{:S(2)}) copy-start(f32[256]{0:T(256)} %param.31) | copy-start | bytes 3076
Sparse Core Ops, SparseCore 0:
  9.5 44.6 all-gather.1
